TPU v7x, 128 devices: a whole 4x4x4 slice. The times are simulated.
128 devices in a mesh: dp: 8 (over y, core), expert: 16 (over z, x).
Axes of the slice: x: 4, y: 4, z: 4, core: 2. Of those that a mesh axis runs over, the one named last changes fastest.
Arguments:
- tokens: bfloat16 [2, 16, 1024, 1024], P(None, 'expert', 'dp'), may hold values from -6 to 6
- cotangent: bfloat16 [2, 16, 1024, 1024], P(None, 'expert', 'dp'), may hold values from -6 to 6
- segments: int32 [2, 16, 1024], P(None, 'expert'), may hold values from 0 to 4, as said below
- routes: int32 [2, 16, 1024, 8], P(None, 'expert', 'dp'), may hold values from 0 to 31, all different within a row; in each aligned block of 128 rows (0 to 127, 128 to 255, ..., all dimensions but the last counted through in order) at most 48 rows name the same one
- w_qkv: bfloat16 [1024, 2048], P('dp'), may hold values from -0.1875 to 0.1875
- w_out: bfloat16 [1024, 1024], P('dp'), may hold values from -0.75 to 0.75
- attn_norm: bfloat16 [1024], P('dp'), may hold values from 0.099609375 to 1.8984375
- ffn_norm: bfloat16 [1024], P('dp'), may hold values from 0.099609375 to 1.8984375
- q_gain: bfloat16 [64], P('dp'), may hold values from 0.099609375 to 1.8984375
- k_gain: bfloat16 [64], P('dp'), may hold values from 0.099609375 to 1.8984375
- router: bfloat16 [1024, 32], P('dp'), may hold values from -0.09375 to 0.09375
- w_gate_up: bfloat16 [32, 1024, 1024], P('expert'), may hold values from -0.1875 to 0.1875
- w_down: bfloat16 [32, 512, 1024], P('expert'), may hold values from -1 to 1
Outputs:
- output: bfloat16 [2, 16, 1024, 1024], P(None, 'expert', 'dp')
- input_grad: bfloat16 [2, 16, 1024, 1024], P(None, 'expert', 'dp')
- grad_qkv: float32 [1024, 2048], P('dp')
- grad_out: float32 [1024, 1024], P('dp')
- grad_attn_norm: float32 [1024], P('dp')
- grad_ffn_norm: float32 [1024], P('dp')
- grad_q_gain: float32 [64], P('dp')
- grad_k_gain: float32 [64], P('dp')
- grad_router: float32 [1024, 32], P('dp')
- grad_gate_up: float32 [32, 1024, 1024], P('expert')
- grad_down: float32 [32, 512, 1024], P('expert')
Inputs may be any that keep to these rules, and one draw needn't show every extreme that they name: `segments`: segment numbers never fall along a sequence; equal numbers mark one document. `routes`: the 8 experts of a token differ. Within each aligned block of 128 positions of one sequence in one micro-batch no expert is named more than 48 times, a bound that some block reaches.
All inputs are finite; a program needn't handle non-finite values.
Results may differ from a plain program's by a relative error of at most 0.025.
Values may be sent and summed in bfloat16 or wider, within the bound.
A program may use at most 256 MiB of HBM per device.

v0:
```python
import jax
import jax.numpy as jnp
import numpy as np
from jax import lax
from jax.experimental import pallas as pl
from jax.experimental.pallas import tpu as pltpu
from jax.sharding import PartitionSpec as P

HD = 64
EPSILON = 1e-06
THETA = 10000.0
MASKED = -1e30

BF = jnp.bfloat16
F32 = jnp.float32
SLOTS = 48
CHUNK = 256
MIB = 1024 * 1024


def nn(a, b):
    return lax.dot_general(a, b, (((1,), (0,)), ((), ())), preferred_element_type=F32)


def nt(a, b):
    return lax.dot_general(a, b, (((1,), (1,)), ((), ())), preferred_element_type=F32)


def tn(a, b):
    return lax.dot_general(a, b, (((0,), (0,)), ((), ())), preferred_element_type=F32)


def send(src, dst, send_sem, recv_sem, device):
    return pltpu.make_async_remote_copy(
        src_ref=src, dst_ref=dst, send_sem=send_sem, recv_sem=recv_sem, device_id=device
    )


def next_to(p):
    return (p + 1) % 4, (p + 3) % 4, (p + 2) % 4


def greet(devices):
    sem = pltpu.get_barrier_semaphore()
    for device in devices:
        pl.semaphore_signal(sem, inc=1, device_id=device)
    pl.semaphore_wait(sem, len(devices))


class Plane:
    def __init__(self):
        self.me = lax.axis_index("expert")
        self.z = self.me // 4
        self.x = self.me % 4

    def own(self, half):
        return (self.x, self.z) if half == 0 else (self.z, self.x)

    def device(self, half, p, q):
        return {"expert": q * 4 + p if half == 0 else p * 4 + q}

    def others(self):
        return [{"expert": (self.me + step) % 16} for step in range(1, 16)]

    def neighbours(self):
        zn, zp, _ = next_to(self.z)
        xn, xp, _ = next_to(self.x)
        return [{"expert": k} for k in (zn * 4 + self.x, zp * 4 + self.x, self.z * 4 + xn, self.z * 4 + xp)]


class Column:
    def __init__(self):
        self.me = lax.axis_index("dp")
        self.y = self.me // 2
        self.c = self.me % 2

    def neighbours(self):
        yn, yp, _ = next_to(self.y)
        return [self.to(yn), self.to(yp), self.other()]

    def to(self, y):
        return {"dp": y * 2 + self.c}

    def other(self):
        return {"dp": self.y * 2 + 1 - self.c}


class PlaneStep:
    def at(self, half, p, q, rows):
        return self.ref.at[q, p, rows] if half == 0 else self.ref.at[p, q, rows]

    def line(self, half, q, rows):
        return self.ref.at[q, :, rows] if half == 0 else self.ref.at[:, q, rows]

    def rows(self, half):
        quarter = self.height // 4
        base = 2 * quarter * half
        return pl.ds(base, 2 * quarter), pl.ds(base, quarter), pl.ds(base + quarter, quarter)


class Gather(PlaneStep):
    def __init__(self, plane, ref, sems, height=128):
        self.plane, self.ref, self.sems, self.height = plane, ref, sems, height

    def message(self, half, i):
        p, q = self.plane.own(half)
        pn, pp, _ = next_to(p)
        qn, qp, _ = next_to(q)
        full, first, second = self.rows(half)
        view, to = [
            lambda: (self.at(half, p, q, full), (pn, q)),
            lambda: (self.at(half, p, q, full), (pp, q)),
            lambda: (self.at(half, pp, q, first), (pn, q)),
            lambda: (self.at(half, pn, q, second), (pp, q)),
            lambda: (self.line(half, q, full), (p, qn)),
            lambda: (self.line(half, q, full), (p, qp)),
            lambda: (self.line(half, qp, first), (p, qn)),
            lambda: (self.line(half, qn, second), (p, qp)),
        ][i]()
        sems = self.sems
        return send(view, view, sems.at[0, half, i], sems.at[1, half, i], self.plane.device(half, *to))

    def step(self, n):
        waits, starts = [
            ((), (0, 1)),
            ((0, 1), (2, 3)),
            ((2, 3), (4, 5)),
            ((4, 5), (6, 7)),
            ((6, 7), ()),
        ][n]
        for half in range(2):
            for i in waits:
                self.message(half, i).wait_recv()
            for i in starts:
                self.message(half, i).start()
        if n == 4:
            for half in range(2):
                for i in range(8):
                    self.message(half, i).wait_send()


class Scatter(PlaneStep):
    def __init__(self, plane, ref, slots, sems, store, free=None, height=128):
        self.plane, self.ref, self.slots, self.sems = plane, ref, slots, sems
        self.store, self.free, self.height = store, free, height

    def message(self, half, i):
        p, q = self.plane.own(half)
        pn, pp, po = next_to(p)
        qn, qp, qo = next_to(q)
        full, first, second = self.rows(half)
        r1, r2, r3, r4 = self.slots
        view, slot, to = [
            lambda: (self.line(half, qo, first), r1.at[half, 0], (p, qn)),
            lambda: (self.line(half, qo, second), r1.at[half, 1], (p, qp)),
            lambda: (self.line(half, qn, full), r2.at[half, 0], (p, qn)),
            lambda: (self.line(half, qp, full), r2.at[half, 1], (p, qp)),
            lambda: (self.at(half, po, q, first), r3.at[half, 0], (pn, q)),
            lambda: (self.at(half, po, q, second), r3.at[half, 1], (pp, q)),
            lambda: (self.at(half, pn, q, full), r4.at[half, 0], (pn, q)),
            lambda: (self.at(half, pp, q, full), r4.at[half, 1], (pp, q)),
        ][i]()
        sems = self.sems
        return send(view, slot, sems.at[0, half, i], sems.at[1, half, i], self.plane.device(half, *to))

    def add_line(self, half, q, part, parts, slots):
        quarter = self.height // 4
        offset = quarter * (2 * half + part)
        groups = quarter * parts // 16

        @pl.loop(0, 4 * groups)
        def _(n):
            j, k = n // groups, n % groups
            rows = pl.ds(pl.multiple_of(offset + k * 16, 16), 16)
            some = pl.ds(pl.multiple_of(k * 16, 16), 16)
            place = (q, j, rows) if half == 0 else (j, q, rows)
            total = self.ref[place].astype(F32)
            for ref, side in slots:
                total += ref[half, side, j, some].astype(F32)
            self.ref[place] = total.astype(BF)

    def add_at(self, half, p, q, part, slot):
        quarter = self.height // 4
        ref, side = slot

        @pl.loop(0, quarter // 16)
        def _(k):
            rows = pl.ds(pl.multiple_of(quarter * (2 * half + part) + k * 16, 16), 16)
            place = (q, p, rows) if half == 0 else (p, q, rows)
            got = ref[half, side, pl.ds(pl.multiple_of(k * 16, 16), 16)].astype(F32)
            self.ref[place] = (self.ref[place].astype(F32) + got).astype(BF)

    def step(self, n):
        r1, r2, r3, r4 = self.slots
        for half in range(2):
            p, q = self.plane.own(half)
            pn, pp, po = next_to(p)
            qn, qp, qo = next_to(q)
            if n == 0:
                self.message(half, 0).start()
                self.message(half, 1).start()
            elif n == 1:
                self.message(half, 0).wait_recv()
                self.add_line(half, qn, 0, 1, [(r1, 0)])
                self.message(half, 2).start()
                self.message(half, 1).wait_recv()
                self.add_line(half, qp, 1, 1, [(r1, 1)])
                self.message(half, 3).start()
            elif n == 2:
                self.message(half, 2).wait_recv()
                self.message(half, 3).wait_recv()
                self.add_line(half, q, 0, 2, [(r2, 0), (r2, 1)])
                self.message(half, 4).start()
                self.message(half, 5).start()
            elif n == 3:
                self.message(half, 4).wait_recv()
                self.add_at(half, pn, q, 0, (r3, 0))
                self.message(half, 6).start()
                self.message(half, 5).wait_recv()
                self.add_at(half, pp, q, 1, (r3, 1))
                self.message(half, 7).start()
            elif n == 4:
                self.message(half, 6).wait_recv()
                self.message(half, 7).wait_recv()

                @pl.loop(0, self.height // 32)
                def _(k):
                    rows = pl.ds(pl.multiple_of(self.height // 2 * half + k * 16, 16), 16)
                    place = (q, p, rows) if half == 0 else (p, q, rows)
                    some = pl.ds(pl.multiple_of(k * 16, 16), 16)
                    total = self.ref[place].astype(F32)
                    total += r4[half, 0, some].astype(F32)
                    total += r4[half, 1, some].astype(F32)
                    self.store(place, rows, total)
        if n == 4:
            for half in range(2):
                for i in range(8):
                    self.message(half, i).wait_send()

    def give_credit(self):
        for device in self.plane.neighbours():
            pl.semaphore_signal(self.free, inc=1, device_id=device)

    def take_credit(self):
        pl.semaphore_wait(self.free, 4)


def scatter_slots(height, width, lead=()):
    quarter = height // 4
    return [
        pltpu.VMEM((*lead, 2, 2, 4, quarter, width), BF),
        pltpu.VMEM((*lead, 2, 2, 4, 2 * quarter, width), BF),
        pltpu.VMEM((*lead, 2, 2, quarter, width), BF),
        pltpu.VMEM((*lead, 2, 2, 2 * quarter, width), BF),
    ]


class ColumnGather:
    def __init__(self, column, ref, sems, count, own=None):
        self.column, self.ref, self.sems, self.count = column, ref, sems, count
        self.own = own

    def message(self, i):
        y, c = self.column.y, self.column.c
        yn, yp, yo = next_to(y)
        half = self.count // 2
        ref, column = self.ref, self.column
        view, device = [
            lambda: (ref.at[y, c], column.to(yn)),
            lambda: (ref.at[y, c], column.to(yp)),
            lambda: (ref.at[y, c], column.other()),
            lambda: (ref.at[yp, c, pl.ds(0, half)], column.to(yn)),
            lambda: (ref.at[yn, c, pl.ds(half, half)], column.to(yp)),
            lambda: (ref.at[yp, c], column.other()),
            lambda: (ref.at[yn, c], column.other()),
            lambda: (ref.at[yo, c], column.other()),
        ][i]()
        source = self.own if i < 3 and self.own is not None else view
        return send(source, view, self.sems.at[0, i], self.sems.at[1, i], device)

    def step(self, n):
        order = [
            [("s", 0), ("s", 1), ("s", 2)],
            [("w", 0), ("s", 3), ("s", 5), ("w", 1), ("s", 4), ("s", 6)],
            [("w", 3), ("w", 4), ("s", 7)],
            [("w", 2), ("w", 5), ("w", 6), ("w", 7)],
        ][n]
        for what, i in order:
            if what == "s":
                self.message(i).start()
            else:
                self.message(i).wait_recv()
        if n == 3:
            for i in range(8):
                self.message(i).wait_send()


class ColumnScatter:
    def __init__(self, column, ref, slots, sems, count, store, group=16):
        self.column, self.ref, self.slots, self.sems = column, ref, slots, sems
        self.count, self.store, self.group = count, store, group

    def message(self, i):
        y, c = self.column.y, self.column.c
        yn, yp, yo = next_to(y)
        half = self.count // 2
        ref, column = self.ref, self.column
        ra, rb, rc = self.slots
        view, slot, device = [
            lambda: (ref.at[:, 1 - c], ra, column.other()),
            lambda: (ref.at[yo, c, pl.ds(0, half)], rb.at[0], column.to(yn)),
            lambda: (ref.at[yo, c, pl.ds(half, half)], rb.at[1], column.to(yp)),
            lambda: (ref.at[yn, c], rc.at[0], column.to(yn)),
            lambda: (ref.at[yp, c], rc.at[1], column.to(yp)),
        ][i]()
        return send(view, slot, self.sems.at[0, i], self.sems.at[1, i], device)

    def some(self, k, base=0):
        return pl.ds(pl.multiple_of(base + k * self.group, self.group), self.group)

    def step(self, n):
        y, c = self.column.y, self.column.c
        yn, yp, yo = next_to(y)
        ref, (ra, rb, rc) = self.ref, self.slots
        low = ref.dtype
        half = self.count // 2
        groups = self.count // self.group
        if n == 0:
            self.message(0).start()
        elif n == 1:
            self.message(0).wait_recv()

            @pl.loop(0, 4 * groups)
            def _(k):
                j, r = k // groups, self.some(k % groups)
                ref[j, c, r] = (ref[j, c, r].astype(F32) + ra[j, r].astype(F32)).astype(low)

            self.message(1).start()
            self.message(2).start()
        elif n == 2:
            for side, to in ((0, yn), (1, yp)):
                self.message(1 + side).wait_recv()

                @pl.loop(0, groups // 2)
                def _(k):
                    r = self.some(k, side * half)
                    got = rb[side, self.some(k)].astype(F32)
                    ref[to, c, r] = (ref[to, c, r].astype(F32) + got).astype(low)

                self.message(3 + side).start()
        else:
            self.message(3).wait_recv()
            self.message(4).wait_recv()

            @pl.loop(0, groups)
            def _(k):
                r = self.some(k)
                total = ref[y, c, r].astype(F32) + rc[0, r].astype(F32) + rc[1, r].astype(F32)
                self.store(r, total)

            for i in range(5):
                self.message(i).wait_send()


def column_slots(shape, dtype=BF, lead=()):
    count, rest = shape[0], shape[1:]
    return [
        pltpu.VMEM((*lead, 4, count, *rest), dtype),
        pltpu.VMEM((*lead, 2, count // 2, *rest), dtype),
        pltpu.VMEM((*lead, 2, count, *rest), dtype),
    ]


def turned(v, cosine, sine):
    a, b = v[:32], v[32:]
    return jnp.concatenate([a * cosine - b * sine, b * cosine + a * sine], axis=0)


def inverse_rms(v, axis):
    return lax.rsqrt(jnp.mean(v * v, axis=axis, keepdims=True) + EPSILON)


def head_gain(small_t, row):
    pieces = [small_t[:, 128 * b : 128 * (b + 1)] for b in range(8)]
    tall = jnp.concatenate([piece.T[:8] for piece in pieces], axis=0)
    return jnp.broadcast_to(tall[:, row : row + 1], (64, 128))


def document_bias(seg_ref, bias, mb, mine):
    own = seg_ref[mb, mine].astype(F32)
    for b in range(8):
        keys = jnp.broadcast_to(seg_ref[mb, b].astype(F32), (128, 128)).T
        bias[mb, 128 * b : 128 * (b + 1)] = jnp.where(keys == own, 0.0, MASKED).astype(bias.dtype)


def pair_columns(ref, mb, g):
    both = ref[mb, pl.ds(pl.multiple_of(g * 128, 128), 128)]
    return jnp.concatenate([both[:64], both[64:]], axis=1)


def front_kernel(
    tok, cot, wq, wo, small, seg_ref, routes_ref, turn_hbm,
    dy_out, x0_out, wq_out, wo_out, kv_out, raw_out,
    small_t, q_t, mix_t, lsum, res, ffn, gates_t, g_all,
    dy_all, x0_all, wq_all, wo_all, kv_all, raw_t, small_all, normed, bias, turn, plane_sems, column_sems,
    sent, gsend, grecv, local,
):
    plane, column = Plane(), Column()
    y, c = column.y, column.c
    copies = [
        pltpu.make_async_copy(small, small_all.at[y, c], local.at[0]),
        pltpu.make_async_copy(wq.at[:, 1024:2048], wq_all.at[1, y, c], local.at[1]),
        pltpu.make_async_copy(wq.at[:, 0:1024], wq_all.at[0, y, c], local.at[3]),
        pltpu.make_async_copy(wo, wo_all.at[y, c], local.at[5]),
        pltpu.make_async_copy(turn_hbm.at[column.me], turn, local.at[6]),
    ]
    for copy in copies:
        copy.start()
    outs = [
        pltpu.make_async_copy(wq_all, wq_out, local.at[7]),
        pltpu.make_async_copy(wo_all, wo_out, local.at[8]),
        pltpu.make_async_copy(kv_all, kv_out, local.at[9]),
        pltpu.make_async_copy(raw_t, raw_out, local.at[10]),
        pltpu.make_async_copy(dy_all.at[0], dy_out.at[0], local.at[11]),
        pltpu.make_async_copy(dy_all.at[1], dy_out.at[1], local.at[2]),
        pltpu.make_async_copy(x0_all, x0_out, local.at[4]),
    ]
    for mb in range(2):
        dy_all[mb, plane.z, plane.x] = cot[mb]
    greet(plane.others() + column.neighbours())
    gdy = [Gather(plane, dy_all.at[mb], plane_sems.at[mb]) for mb in range(2)]
    gx = Gather(plane, x0_all, plane_sems.at[2])
    w_small = ColumnGather(column, small_all, column_sems.at[0], 64)
    w_q = ColumnGather(column, wq_all.at[0], column_sems.at[1], 128)
    w_kv = ColumnGather(column, wq_all.at[1], column_sems.at[2], 128)
    w_o = ColumnGather(column, wo_all, column_sems.at[3], 128)
    kv = [ColumnGather(column, kv_all.at[mb], column_sems.at[4 + mb], 8) for mb in range(2)]
    def both_biases():
        for mb in range(2):
            document_bias(seg_ref, bias, mb, column.me)

    def norm_tokens():
        for b in range(8):
            small_t[:, 128 * b : 128 * (b + 1)] = small_all[b // 2, b % 2].astype(F32)
        attn_gain = small_t[32:33]
        for mb in range(2):
            v = tok[mb].astype(F32)
            normed[128 * mb : 128 * (mb + 1)] = (v * inverse_rms(v, 1) * attn_gain).astype(BF)

    def project(k):
        @pl.loop(0, 2)
        def _(n):
            cols = pl.ds(pl.multiple_of(n * 512, 512), 512)
            rows = pl.ds(pl.multiple_of(1024 * k + n * 512, 512), 512)
            got = nn(normed[...], wq_all[k, :, :, :, cols].reshape(1024, 512))
            for mb in range(2):
                raw_t[mb, rows] = got[128 * mb : 128 * (mb + 1)].T

    def key_heads(mb):
        @pl.loop(0, 8)
        def _(g):
            v = raw_t[mb, pl.ds(pl.multiple_of(1024 + g * 64, 64), 64)]
            key = turned(v * inverse_rms(v, 0) * key_gain, cosine, sine)
            value = raw_t[mb, pl.ds(pl.multiple_of(1536 + g * 64, 64), 64)]
            kv_all[mb, y, c, g] = jnp.concatenate([key, value], axis=0).T.astype(BF)

    def query_heads(mb):
        @pl.loop(0, 16)
        def _(h):
            rows = pl.ds(pl.multiple_of(h * 64, 64), 64)
            v = raw_t[mb, rows]
            query = turned(v * inverse_rms(v, 0) * query_gain, cosine, sine)
            q_t[mb, rows] = (query.astype(BF).astype(F32) * HD ** (-0.5)).astype(BF)

    def attend(mb, start, stop):
        @pl.loop(start, stop)
        def _(g):
            query = pair_columns(q_t, mb, g)
            query = jnp.concatenate([query, jnp.zeros_like(query)], axis=0)
            total = jnp.zeros((1, 256), F32)
            mixed = jnp.zeros((128, 256), F32)
            for j in range(4):
                keys = kv_all[mb, j, :, g].reshape(256, 128)
                there = bias[mb, 256 * j : 256 * (j + 1)].astype(F32)
                p = jnp.exp(nn(keys, query) + jnp.concatenate([there, there], axis=1))
                total += jnp.sum(p, axis=0, keepdims=True)
                mixed += tn(keys, p.astype(BF))
            lsum[mb, g] = total
            mixed = (mixed[64:] / total).astype(BF)
            both = jnp.concatenate([mixed[:, :128], mixed[:, 128:]], axis=0)
            mix_t[mb, pl.ds(pl.multiple_of(g * 128, 128), 128)] = both

    def finish(mb):
        @pl.loop(0, 2)
        def _(n):
            cols = pl.ds(pl.multiple_of(n * 512, 512), 512)
            got = tn(mix_t[mb], wo_all[:, :, :, cols].reshape(1024, 512))
            res[mb, :, cols] = tok[mb, :, cols].astype(F32) + got

        v = res[mb]
        low = (v * inverse_rms(v, 1) * small_t[33:34]).astype(BF)
        ffn[mb] = low
        logits = nt(small_t[:32].astype(BF), low)
        ids = lax.broadcasted_iota(jnp.int32, (32, 128), 0)
        routed = ids == routes_ref[mb, 0:1]
        for k in range(1, 8):
            routed = routed | (ids == routes_ref[mb, k : k + 1])
        top = jnp.max(jnp.where(routed, logits, MASKED), axis=0, keepdims=True)
        weight = jnp.where(routed, jnp.exp(logits - top), 0.0)
        gates = weight / jnp.sum(weight, axis=0, keepdims=True)
        gates_t[mb] = gates
        for k in range(16):
            sent[k, 2 * mb : 2 * mb + 2] = gates[2 * k : 2 * k + 2]

    def gate_message(step):
        to = (plane.me + step) % 16
        return send(
            sent.at[to], g_all.at[plane.me], gsend.at[step], grecv.at[step], {"expert": to}
        )

    def send_gates():
        for step in range(1, 16):
            gate_message(step).start()
        g_all[plane.me] = sent[plane.me]

    def take_gates():
        for step in range(1, 16):
            gate_message(step).wait_recv()
        for step in range(1, 16):
            gate_message(step).wait_send()

    sent[...] = jnp.zeros_like(sent)
    copies[0].wait()
    w_small.step(0)
    gdy[0].step(0)
    copies[1].wait()
    w_kv.step(0)
    w_small.step(1)
    gdy[1].step(0)
    copies[2].wait()
    w_q.step(0)
    gdy[0].step(1)
    gdy[0].step(2)
    w_small.step(2)
    w_kv.step(1)
    gdy[1].step(1)
    w_q.step(1)
    copies[3].wait()
    w_o.step(0)
    w_small.step(3)
    norm_tokens()
    w_kv.step(2)
    w_kv.step(3)
    project(1)
    gdy[1].step(2)
    query_gain = head_gain(small_t[...], 34)
    key_gain = head_gain(small_t[...], 35)
    copies[4].wait()
    cosine, sine = turn[:32], turn[32:]
    key_heads(0)
    kv[0].step(0)
    kv[0].step(1)
    both_biases()
    key_heads(1)
    w_q.step(2)
    gdy[0].step(3)
    w_o.step(1)
    kv[0].step(2)
    w_q.step(3)
    outs[0].start()
    project(0)
    outs[3].start()
    kv[1].step(0)
    w_o.step(2)
    gdy[1].step(3)
    query_heads(0)
    kv[0].step(3)
    attend(0, 0, 4)
    attend(0, 4, 8)
    w_o.step(3)
    outs[1].start()
    finish(0)
    x0_all[plane.z, plane.x] = ffn[0]
    gx.step(0)
    query_heads(1)
    kv[1].step(1)
    gx.step(1)
    kv[1].step(2)
    gdy[1].step(4)
    outs[5].start()
    gx.step(2)
    kv[1].step(3)
    outs[2].start()
    attend(1, 0, 4)
    gx.step(3)
    attend(1, 4, 8)
    finish(1)
    send_gates()
    gdy[0].step(4)
    outs[4].start()
    take_gates()
    gx.step(4)
    outs[6].start()
    for copy in outs:
        copy.wait()


def front(tok, cot, wq, wo, small, seg, routes_t, turn):
    vmem = pl.BlockSpec(memory_space=pltpu.VMEM)
    anywhere = pl.BlockSpec(memory_space=pl.ANY)
    return pl.pallas_call(
        front_kernel,
        out_shape=(
            jax.ShapeDtypeStruct((2, 4, 4, 128, 1024), BF),
            jax.ShapeDtypeStruct((4, 4, 128, 1024), BF),
            jax.ShapeDtypeStruct((2, 4, 2, 128, 1024), BF),
            jax.ShapeDtypeStruct((4, 2, 128, 1024), BF),
            jax.ShapeDtypeStruct((2, 4, 2, 8, 128, 128), BF),
            jax.ShapeDtypeStruct((2, 2048, 128), F32),
            jax.ShapeDtypeStruct((64, 1024), F32),
            jax.ShapeDtypeStruct((2, 1024, 128), BF),
            jax.ShapeDtypeStruct((2, 1024, 128), BF),
            jax.ShapeDtypeStruct((2, 8, 1, 256), F32),
            jax.ShapeDtypeStruct((2, 128, 1024), F32),
            jax.ShapeDtypeStruct((2, 128, 1024), BF),
            jax.ShapeDtypeStruct((2, 32, 128), F32),
            jax.ShapeDtypeStruct((16, 8, 128), F32),
        ),
        in_specs=[vmem, vmem, anywhere, anywhere, anywhere, vmem, vmem, anywhere],
        out_specs=(anywhere,) * 6 + (vmem,) * 8,
        scratch_shapes=[
            pltpu.VMEM((2, 4, 4, 128, 1024), BF),
            pltpu.VMEM((4, 4, 128, 1024), BF),
            pltpu.VMEM((2, 4, 2, 128, 1024), BF),
            pltpu.VMEM((4, 2, 128, 1024), BF),
            pltpu.VMEM((2, 4, 2, 8, 128, 128), BF),
            pltpu.VMEM((2, 2048, 128), F32),
            pltpu.VMEM((4, 2, 64, 128), BF),
            pltpu.VMEM((256, 1024), BF),
            pltpu.VMEM((2, 1024, 128), F32),
            pltpu.VMEM((64, 128), F32),
            pltpu.SemaphoreType.DMA((3, 2, 2, 8)),
            pltpu.SemaphoreType.DMA((6, 2, 8)),
            pltpu.VMEM((16, 8, 128), F32),
            pltpu.SemaphoreType.DMA((16,)),
            pltpu.SemaphoreType.DMA((16,)),
            pltpu.SemaphoreType.DMA((12,)),
        ],
        compiler_params=pltpu.CompilerParams(
            collective_id=0, has_side_effects=True, vmem_limit_bytes=56 * MIB
        ),
        cost_estimate=pl.CostEstimate(
            flops=5_000_000_000, bytes_accessed=30_000_000, transcendentals=5_000_000
        ),
    )(tok, cot, wq, wo, small, seg, routes_t, turn)


def moe_kernel(
    ffn_ref, x0_hbm, dy_hbm, g_all, wgu_hbm, wd_hbm,
    out_hbm, dx_ref, h_ref, dw_own,
    dw, x_all, dy_all, r1, r2, r3, r4, xs, ds, os, gc, act, a1, a2, ggu, ranks, hcol, hs,
    wgu, wd, ra, rb, rc, sems, column_sems, hsend, hrecv, free, local,
):
    plane, column = Plane(), Column()
    me, z, x = plane.me, plane.z, plane.x
    own = [
        pltpu.make_async_copy(ffn_ref.at[1], x_all.at[1, z, x], local.at[0]),
        pltpu.make_async_copy(x0_hbm, x_all.at[0], local.at[2]),
        pltpu.make_async_copy(dy_hbm.at[0], dy_all.at[0], local.at[3]),
        pltpu.make_async_copy(wgu_hbm, wgu, local.at[4]),
        pltpu.make_async_copy(wd_hbm, wd, local.at[5]),
        pltpu.make_async_copy(dy_hbm.at[1], dy_all.at[1], local.at[1]),
    ]
    outs = [pltpu.make_async_copy(x_all.at[mb], out_hbm.at[mb], local.at[6 + mb]) for mb in range(2)]
    for copy in own:
        copy.start()
    greet(plane.others() + column.neighbours())
    own[0].wait()

    def h_message(step):
        to = (me + step) % 16
        return pltpu.make_async_remote_copy(
            src_ref=hs.at[to], dst_ref=h_ref.at[me],
            send_sem=hsend.at[step], recv_sem=hrecv.at[step], device_id={"expert": to},
        )

    gx = Gather(plane, x_all.at[1], sems.at[0])

    def into(mb):
        def store(place, rows, total):
            dx_ref[mb, rows] = total

        return store

    sdx = [
        Scatter(plane, dy_all.at[mb], (r1, r2, r3, r4), sems.at[1 + mb], into(mb), free)
        for mb in range(2)
    ]

    def own_part(k):
        def store(r, total):
            dw_own[k, r] = total.astype(BF)

        return store

    dsum = [
        ColumnScatter(
            column, dw.at[k], (ra.at[k], rb.at[k], rc.at[k]), column_sems.at[k], 128, own_part(k)
        )
        for k in range(3)
    ]
    earlier = (
        lax.broadcasted_iota(jnp.int32, (128, 128), 0)
        < lax.broadcasted_iota(jnp.int32, (128, 128), 1)
    ).astype(F32).astype(BF)

    @pl.loop(0, 16)
    def _(s):
        named = g_all[s] > 0.0
        before = nn(named.astype(F32).astype(BF), earlier)
        ranks[s] = jnp.where(named, before, -1.0)

    slot_ids = lax.broadcasted_iota(jnp.int32, (SLOTS, 128), 0).astype(F32)

    def places(p, mb):
        ranked = [ranks[2 * p + k] for k in range(2)]
        return [
            [(slot_ids == ranked[k][2 * mb + e : 2 * mb + e + 1]).astype(F32) for k in range(2)]
            for e in range(2)
        ]

    def gated(p, mb, hot):
        gates = [g_all[2 * p + k] for k in range(2)]
        return [
            [hot[e][k] * gates[k][2 * mb + e : 2 * mb + e + 1] for k in range(2)] for e in range(2)
        ]

    def spread(hot):
        blank = jnp.zeros((SLOTS, 128), F32)
        rows = []
        for e in range(2):
            rows.append(jnp.concatenate([hot[e][0], blank], axis=1))
            rows.append(jnp.concatenate([blank, hot[e][1]], axis=1))
        return jnp.concatenate(rows, axis=0).astype(BF)

    def span(p):
        return pl.ds(pl.multiple_of(p * 2 * SLOTS, 32), 2 * SLOTS)

    def pair(p):
        return p // 2, pl.ds(2 * (p % 2), 2)

    def select(mb):
        @pl.loop(0, 8)
        def _(p):
            hot = places(p, mb)
            line, two = pair(p)
            rows = nn(spread(hot), x_all[mb, line, two].reshape(256, 1024)).astype(BF)
            drows = nn(spread(gated(p, mb, hot)), dy_all[mb, line, two].reshape(256, 1024)).astype(BF)
            for e in range(2):
                xs[e, span(p)] = rows[2 * SLOTS * e : 2 * SLOTS * (e + 1)]
                ds[e, span(p)] = drows[2 * SLOTS * e : 2 * SLOTS * (e + 1)]

    chunks = 16 * SLOTS // CHUNK

    def forward(e):
        @pl.loop(0, chunks)
        def _(c):
            r = pl.ds(pl.multiple_of(c * CHUNK, CHUNK), CHUNK)
            gu = nn(xs[e, r], wgu[e])
            g, u = gu[:, :512], gu[:, 512:]
            sig = 1.0 / (1.0 + jnp.exp(-g))
            silu = g * sig
            active = (silu * u).astype(BF)
            act[e, r] = active
            a1[e, r] = (u * sig * (1.0 + g * (1.0 - sig))).astype(BF)
            a2[e, r] = silu.astype(BF)
            o = nn(active, wd[e]).astype(BF)
            os[e, r] = o
            hcol[e, r] = jnp.sum(o.astype(F32) * ds[e, r].astype(F32), axis=-1, keepdims=True)

    def combine_out(mb):
        @pl.loop(0, 8)
        def _(p):
            hot = places(p, mb)
            line, two = pair(p)
            both = jnp.concatenate([os[0, span(p)], os[1, span(p)]], axis=0)
            got = tn(spread(gated(p, mb, hot)), both).astype(BF)
            x_all[mb, line, two] = got.reshape(2, 128, 1024)
            for e in range(2):
                column_of = hcol[e, span(p)]
                for k in range(2):
                    row = 2 * mb + e
                    part = hot[e][k] * column_of[SLOTS * k : SLOTS * (k + 1)]
                    hs[2 * p + k, row : row + 1] = jnp.sum(part, axis=0, keepdims=True)

    def add_part(mb, k, n, fresh):
        fresh = fresh.reshape(2, 128, 1024)
        if mb == 1:
            fresh += dw[k, n].astype(F32)
        dw[k, n] = fresh.astype(BF)

    def backward(mb, e):
        @pl.loop(0, chunks)
        def _(c):
            r = pl.ds(pl.multiple_of(c * CHUNK, CHUNK), CHUNK)
            ga = nt(ds[e, r], wd[e])
            grad = jnp.concatenate(
                [ga * a1[e, r].astype(F32), ga * a2[e, r].astype(F32)], axis=1
            ).astype(BF)
            ggu[r] = grad
            gc[e, r] = nt(grad, wgu[e]).astype(BF)

        @pl.loop(0, 4)
        def _(m):
            cols = pl.ds(pl.multiple_of(m * 256, 256), 256)
            add_part(mb, e, m, tn(xs[e, :, cols], ggu[...]))

        @pl.loop(0, 2)
        def _(m):
            cols = pl.ds(pl.multiple_of(m * 256, 256), 256)
            add_part(mb, 2, 2 * e + m, tn(act[e, :, cols], ds[e]))

    def combine_dx(mb):
        @pl.loop(0, 8)
        def _(p):
            line, two = pair(p)
            both = jnp.concatenate([gc[0, span(p)], gc[1, span(p)]], axis=0)
            got = tn(spread(places(p, mb)), both).astype(BF)
            dy_all[mb, line, two] = got.reshape(2, 128, 1024)

    gx.step(0)
    own[1].wait()
    own[2].wait()
    select(0)
    gx.step(1)
    own[3].wait()
    own[4].wait()
    forward(0)
    gx.step(2)
    forward(1)
    combine_out(0)
    outs[0].start()
    backward(0, 0)
    gx.step(3)
    backward(0, 1)
    combine_dx(0)
    sdx[0].step(0)
    gx.step(4)
    own[5].wait()
    select(1)
    forward(1)
    sdx[0].step(1)
    forward(0)
    backward(1, 0)
    dsum[0].step(0)
    sdx[0].step(2)
    backward(1, 1)
    sdx[0].step(3)
    dsum[1].step(0)
    dsum[2].step(0)
    dsum[0].step(1)
    combine_dx(1)
    sdx[0].step(4)
    sdx[0].give_credit()
    sdx[1].take_credit()
    sdx[1].step(0)
    dsum[2].step(1)
    combine_out(1)
    outs[1].start()
    dsum[1].step(1)
    sdx[1].step(1)
    dsum[0].step(2)
    dsum[1].step(2)
    dsum[2].step(2)
    sdx[1].step(2)
    h_ref[me] = hs[me]
    for step in range(1, 16):
        h_message(step).start()
    sdx[1].step(3)
    dsum[0].step(3)
    dsum[2].step(3)
    dsum[1].step(3)
    sdx[1].step(4)
    for step in range(1, 16):
        h_message(step).wait_recv()
    for step in range(1, 16):
        h_message(step).wait_send()
    for copy in outs:
        copy.wait()


def moe(ffn, x0, dy, gates, w_gate_up, w_down):
    vmem = pl.BlockSpec(memory_space=pltpu.VMEM)
    anywhere = pl.BlockSpec(memory_space=pl.ANY)
    rows = 16 * SLOTS
    return pl.pallas_call(
        moe_kernel,
        out_shape=(
            jax.ShapeDtypeStruct((2, 4, 4, 128, 1024), BF),
            jax.ShapeDtypeStruct((2, 128, 1024), F32),
            jax.ShapeDtypeStruct((16, 8, 128), F32),
            jax.ShapeDtypeStruct((3, 128, 1024), BF),
        ),
        in_specs=[anywhere, anywhere, anywhere, vmem, anywhere, anywhere],
        out_specs=(anywhere,) + (vmem,) * 3,
        scratch_shapes=[
            pltpu.VMEM((3, 4, 2, 128, 1024), BF),
            pltpu.VMEM((2, 4, 4, 128, 1024), BF),
            pltpu.VMEM((2, 4, 4, 128, 1024), BF),
            *scatter_slots(128, 1024),
            pltpu.VMEM((2, rows, 1024), BF),
            pltpu.VMEM((2, rows, 1024), BF),
            pltpu.VMEM((2, rows, 1024), BF),
            pltpu.VMEM((2, rows, 1024), BF),
            pltpu.VMEM((2, rows, 512), BF),
            pltpu.VMEM((2, rows, 512), BF),
            pltpu.VMEM((2, rows, 512), BF),
            pltpu.VMEM((rows, 1024), BF),
            pltpu.VMEM((16, 8, 128), F32),
            pltpu.VMEM((2, rows, 1), F32),
            pltpu.VMEM((16, 8, 128), F32),
            pltpu.VMEM((2, 1024, 1024), BF),
            pltpu.VMEM((2, 512, 1024), BF),
            *column_slots((128, 1024), lead=(3,)),
            pltpu.SemaphoreType.DMA((3, 2, 2, 8)),
            pltpu.SemaphoreType.DMA((3, 2, 8)),
            pltpu.SemaphoreType.DMA((16,)),
            pltpu.SemaphoreType.DMA((16,)),
            pltpu.SemaphoreType.REGULAR,
            pltpu.SemaphoreType.DMA((8,)),
        ],
        compiler_params=pltpu.CompilerParams(
            collective_id=1, has_side_effects=True, vmem_limit_bytes=63 * MIB
        ),
        cost_estimate=pl.CostEstimate(
            flops=30_000_000_000, bytes_accessed=30_000_000, transcendentals=2_000_000
        ),
    )(ffn, x0, dy, gates, w_gate_up, w_down)


def norm_grad(grad, v, inverse, gain, axis):
    scaled = grad * gain
    moment = jnp.mean(scaled * v, axis=axis, keepdims=True)
    return inverse * (scaled - v * (inverse * inverse * moment)), grad * (v * inverse)


def back_kernel(
    tok, cot, seg_ref, turn_hbm, wq_hbm, wo_hbm, small_t, raw_hbm, q_t, kv_hbm, mix_t, lsum,
    res, ffn, gates_t, share_ref, dx, out_hbm, dw_own,
    dgu_all, dd_all, output, in_grad, gq, go, gs,
    wq_all, wo_all, kv_all, raw_t, turn, bias, gres, branch, gm_t, dq_t, own_kv, gp, normed_t, gn,
    part_kv, part_w, part_s, q_sum, k_sum, ra, rb, rc, sa, sb, sc, plane_buf, plane_all, p1, p2, p3, p4, ta, tb, tc,
    logits, routers, router_sum, out_part, r1, r2, r3, r4, parcels, got_parcels, small_own, kv_total,
    column_sems, plane_sems, far_send, far_recv, all_send, all_recv, free, local, gain_sums,
):
    plane, column = Plane(), Column()
    y, c = column.y, column.c
    copies = [
        pltpu.make_async_copy(wo_hbm, wo_all, local.at[0]),
        pltpu.make_async_copy(kv_hbm, kv_all, local.at[1]),
        pltpu.make_async_copy(raw_hbm, raw_t, local.at[2]),
        pltpu.make_async_copy(wq_hbm, wq_all, local.at[3]),
        pltpu.make_async_copy(turn_hbm.at[column.me], turn, local.at[4]),
    ]
    parts = [pltpu.make_async_copy(out_hbm.at[mb], out_part, local.at[5 + mb]) for mb in range(2)]
    dw_refs = [dgu_all.at[0], dgu_all.at[1], dd_all]
    owns = [pltpu.make_async_copy(dw_own.at[n], dw_refs[n].at[y, c], local.at[7 + n]) for n in range(3)]
    for copy in parts[:1] + owns + copies:
        copy.start()
    greet(plane.others() + column.neighbours())
    dall = [ColumnGather(column, dw_refs[n], column_sems.at[8 + n], 128, dw_own.at[n]) for n in range(3)]

    def add_residual(mb):
        def store(place, rows, total):
            output[mb, rows] = (res[mb, rows] + total).astype(BF)

        return store

    sout = [
        Scatter(plane, out_part, (r1, r2, r3, r4), plane_sems.at[mb], add_residual(mb), free)
        for mb in range(2)
    ]
    part_s[...] = jnp.zeros_like(part_s)
    q_sum[...] = jnp.zeros_like(q_sum)
    k_sum[...] = jnp.zeros_like(k_sum)
    for mb in range(2):
        document_bias(seg_ref, bias, mb, column.me)

    def place_w(which):
        def store(r, total):
            low = total.astype(BF)
            half = r.start // 64
            some = pl.ds(pl.multiple_of(r.start % 64, 16), 16)
            for k in range(8):
                n = half * 8 + k
                piece = low[:, 128 * k : 128 * (k + 1)]
                if which == 2:
                    parcels[n, some] = piece
                else:
                    plane_buf[n // 4, n % 4, some, 128 * which : 128 * (which + 1)] = piece

        return store

    def place_s(r, total):
        small_own[r] = total.astype(BF)

    def place_kv(mb, half):
        def store(r, total):
            own_kv[mb, pl.ds(r.start + 4 * half, 1)] = total

        return store

    w_sums = [
        ColumnScatter(
            column, part_w.at[n], (ra.at[n], rb.at[n], rc.at[n]), column_sems.at[n], 128, place_w(n)
        )
        for n in range(3)
    ]
    kv_sums = [
        [
            ColumnScatter(
                column, part_kv.at[mb, half],
                (sa.at[mb, half], sb.at[mb, half], sc.at[mb, half]),
                column_sems.at[4 + 2 * mb + half], 4, place_kv(mb, half), group=1,
            )
            for half in range(2)
        ]
        for mb in range(2)
    ]
    s_sum = ColumnScatter(column, part_s, (ta, tb, tc), column_sems.at[3], 64, place_s)

    def keep(place, rows, total):
        plane_all[place] = total.astype(BF)

    over = Scatter(plane, plane_buf, (p1, p2, p3, p4), plane_sems.at[2], keep, height=64)
    spread = Gather(plane, plane_all, plane_sems.at[3], height=64)

    def tokens_of(mb):
        return pl.ds(128 * mb, 128)

    router = small_t[:32].astype(BF)
    ffn_gain, attn_gain = small_t[33:34], small_t[32:33]
    routers[0:32] = router
    routers[32:64] = router
    def router_and_norm():
        ffn_gain_grad = jnp.zeros((1, 1024), F32)
        for mb in range(2):
            share = jnp.concatenate([share_ref[k, 2 * mb : 2 * mb + 2] for k in range(16)], axis=0)
            logit = share - gates_t[mb] * jnp.sum(share, axis=0, keepdims=True)
            high = logit.astype(BF)
            logits[0:32, tokens_of(mb)] = high
            logits[32:64, tokens_of(mb)] = (logit - high.astype(F32)).astype(BF)

        @pl.loop(0, 4)
        def _(n):
            cols = pl.ds(pl.multiple_of(n * 256, 256), 256)
            gn[:, cols] = tn(logits[...], routers[:, cols])
            router_sum[:, cols] = nn(logits[...], ffn[:, :, cols].reshape(256, 256))

        for mb in range(2):
            into = dx[mb] + gn[tokens_of(mb)]
            v = res[mb]
            inv = inverse_rms(v, 1)
            grad, gain = norm_grad(into, v, inv, ffn_gain, 1)
            ffn_gain_grad += jnp.sum(gain, axis=0, keepdims=True)
            total = cot[mb].astype(F32) + grad
            gres[mb] = total
            branch[128 * mb : 128 * (mb + 1)] = total.astype(BF)
        gain_sums[1:2] = ffn_gain_grad

    def out_projection():
        copies[0].wait()

        @pl.loop(0, 4)
        def _(n):
            rows = pl.ds(pl.multiple_of(n * 256, 256), 256)
            got = nt(wo_all[n].reshape(256, 1024), branch[...])
            gm_t[0, rows] = got[:, :128].astype(BF)
            gm_t[1, rows] = got[:, 128:].astype(BF)
            mixed = jnp.concatenate([mix_t[0, rows], mix_t[1, rows]], axis=1)
            part_w[0, n] = nn(mixed, branch[...]).astype(BF).reshape(2, 128, 1024)

    def attend(mb, start, stop):
        @pl.loop(start, stop)
        def _(g):
            query = pair_columns(q_t, mb, g)
            grad = pair_columns(gm_t, mb, g)
            mixed = pair_columns(mix_t, mb, g)
            blank = jnp.zeros_like(query)
            inner = jnp.sum(grad.astype(F32) * mixed.astype(F32), axis=0, keepdims=True)
            query = jnp.concatenate([query, blank], axis=0)
            grad = jnp.concatenate([blank, grad], axis=0)
            both = jnp.concatenate([query, grad], axis=1)
            scale = 1.0 / lsum[mb, g]
            dq = jnp.zeros((128, 256), F32)
            for j in range(4):
                keys = kv_all[mb, j, :, g].reshape(256, 128)
                there = bias[mb, 256 * j : 256 * (j + 1)].astype(F32)
                got = nn(keys, both)
                p = jnp.exp(got[:, :256] + jnp.concatenate([there, there], axis=1)) * scale
                ds = (p * (got[:, 256:] - inner)).astype(BF)
                dq += tn(keys, ds)
                dkv = nt(jnp.concatenate([ds, p.astype(BF)], axis=1), both)
                part_kv[mb, g // 4, j, :, g % 4] = dkv.astype(BF).reshape(2, 128, 128)
            dq = dq[:64] * HD ** (-0.5)
            rows = pl.ds(pl.multiple_of(g * 128, 128), 128)
            dq_t[mb, rows] = jnp.concatenate([dq[:, :128], dq[:, 128:]], axis=0)

    copies[4].wait()
    cosine, sine = turn[:32], turn[32:]
    query_gain = head_gain(small_t[...], 34)
    key_gain = head_gain(small_t[...], 35)

    def head_back(grad, v, gain, total):
        inv = inverse_rms(v, 0)
        grad = turned(grad, cosine, -sine)
        grad_v, gain_part = norm_grad(grad, v, inv, gain, 0)
        total[...] += gain_part
        return grad_v

    def queries_back(mb):
        @pl.loop(0, 8)
        def _(g):
            pieces = []
            for r in range(2):
                rows = pl.ds(pl.multiple_of(g * 128 + r * 64, 64), 64)
                pieces.append(head_back(dq_t[mb, rows], raw_t[mb, rows], query_gain, q_sum))
            cols = pl.ds(pl.multiple_of(g * 128, 128), 128)
            gp[tokens_of(mb), cols] = jnp.concatenate(pieces, axis=0).T.astype(BF)

    def turn_normed():
        for mb in range(2):
            v = tok[mb].astype(F32)
            normed = (v * inverse_rms(v, 1) * attn_gain).astype(BF).astype(F32)
            for k in range(8):
                normed_t[128 * k : 128 * (k + 1), tokens_of(mb)] = (
                    normed[:, 128 * k : 128 * (k + 1)].T.astype(BF)
                )

    def weight_part(which):
        cols = pl.ds(1024 * (which - 1), 1024)

        @pl.loop(0, 4)
        def _(n):
            rows = pl.ds(pl.multiple_of(n * 256, 256), 256)
            part_w[which, n] = nn(normed_t[rows], gp[:, cols]).astype(BF).reshape(2, 128, 1024)

    def keys_back(mb):
        @pl.loop(0, 4)
        def _(k):
            keys, values = [], []
            for r in range(2):
                g = 2 * k + r
                grad = own_kv[mb, g].T
                rows = pl.ds(pl.multiple_of(1024 + g * 64, 64), 64)
                keys.append(head_back(grad[:64], raw_t[mb, rows], key_gain, k_sum))
                values.append(grad[64:])
            cols = pl.ds(pl.multiple_of(1024 + k * 128, 128), 128)
            gp[tokens_of(mb), cols] = jnp.concatenate(keys, axis=0).T.astype(BF)
            cols = pl.ds(pl.multiple_of(1536 + k * 128, 128), 128)
            gp[tokens_of(mb), cols] = jnp.concatenate(values, axis=0).T.astype(BF)

    def normed_grad(k):
        @pl.loop(0, 4)
        def _(n):
            cols = pl.ds(pl.multiple_of(n * 256, 256), 256)
            got = nt(gp[:, 1024 * k : 1024 * (k + 1)], wq_all[k, n].reshape(256, 1024))
            gn[:, cols] = got if k == 0 else gn[:, cols] + got

    def finish():
        attn_gain_grad = jnp.zeros((1, 1024), F32)
        for mb in range(2):
            v = tok[mb].astype(F32)
            grad, gain = norm_grad(gn[tokens_of(mb)], v, inverse_rms(v, 1), attn_gain, 1)
            attn_gain_grad += jnp.sum(gain, axis=0, keepdims=True)
            in_grad[mb] = (gres[mb] + grad).astype(BF)
        for b in range(8):
            cols = slice(128 * b, 128 * (b + 1))
            heads = slice(8 * b, 8 * (b + 1))
            part_s[b // 2, b % 2, 0:32] = router_sum[0:32, cols] + router_sum[32:64, cols]
            part_s[b // 2, b % 2, 32:33] = attn_gain_grad[:, cols]
            part_s[b // 2, b % 2, 33:34] = gain_sums[1:2, cols]
            part_s[b // 2, b % 2, 40:48] = jnp.broadcast_to(
                jnp.sum(q_sum[heads], axis=1, keepdims=True), (8, 128)
            )
            part_s[b // 2, b % 2, 48:56] = jnp.broadcast_to(
                jnp.sum(k_sum[heads], axis=1, keepdims=True), (8, 128)
            )

    me = plane.me

    def parcel(step):
        to = (me + step) % 16
        return send(
            parcels.at[to], got_parcels.at[me], far_send.at[step], far_recv.at[step], {"expert": to}
        )

    def total_message(step):
        to = (me + step) % 16
        return send(
            kv_total.at[me], kv_total.at[me], all_send.at[step], all_recv.at[step], {"expert": to}
        )

    def send_parcels():
        @pl.loop(0, 16)
        def _(n):
            parcels[n, 64:128] = small_own[...]

        for step in range(1, 16):
            parcel(step).start()
        got_parcels[me] = parcels[me]

    def add_parcels():
        for step in range(1, 16):
            parcel(step).wait_recv()
        total = got_parcels[0].astype(F32)
        for n in range(1, 16):
            total += got_parcels[n].astype(F32)
        kv_total[me] = total[:64].astype(BF)
        for step in range(1, 16):
            total_message(step).start()
        gs[...] = total[64:]

    def write_out(k):
        for n in range(16):
            rows = slice(64 * (n // 8), 64 * (n // 8) + 64)
            cols = slice(128 * (n % 8), 128 * (n % 8) + 128)
            (go, gq)[k][rows, cols] = plane_all[n // 4, n % 4, :, 128 * k : 128 * (k + 1)].astype(F32)

    def take_totals():
        for step in range(1, 16):
            total_message(step).wait_recv()
        for n in range(16):
            first = 1024 + 128 * (n % 8)
            gq[64 * (n // 8) : 64 * (n // 8) + 64, first : first + 128] = kv_total[n].astype(F32)

    dall[2].step(0)
    router_and_norm()
    parts[0].wait()
    sout[0].step(0)
    dall[0].step(0)
    out_projection()
    dall[1].step(0)
    copies[1].wait()
    attend(1, 0, 2)
    attend(1, 2, 4)
    attend(0, 0, 2)
    kv_sums[1][0].step(0)
    w_sums[0].step(0)
    sout[0].step(1)
    attend(1, 4, 6)
    attend(1, 6, 8)
    dall[0].step(1)
    kv_sums[1][0].step(1)
    kv_sums[1][1].step(0)
    attend(0, 2, 4)
    w_sums[0].step(1)
    attend(0, 4, 6)
    dall[2].step(1)
    kv_sums[1][1].step(1)
    sout[0].step(2)
    w_sums[0].step(2)
    attend(0, 6, 8)
    sout[0].step(3)
    kv_sums[0][1].step(0)
    kv_sums[0][0].step(0)
    kv_sums[1][1].step(2)
    turn_normed()
    copies[2].wait()
    queries_back(1)
    queries_back(0)
    kv_sums[1][0].step(2)
    kv_sums[0][1].step(1)
    weight_part(1)
    copies[3].wait()
    normed_grad(0)
    sout[0].step(4)
    parts[1].start()
    sout[0].give_credit()
    w_sums[1].step(0)
    kv_sums[0][0].step(1)
    kv_sums[0][1].step(2)
    parts[1].wait()
    sout[1].take_credit()
    sout[1].step(0)
    dall[0].step(2)
    w_sums[1].step(1)
    kv_sums[1][1].step(3)
    kv_sums[0][1].step(3)
    kv_sums[0][0].step(2)
    w_sums[1].step(2)
    sout[1].step(1)
    kv_sums[0][0].step(3)
    kv_sums[1][0].step(3)
    keys_back(0)
    dall[2].step(2)
    keys_back(1)
    dall[1].step(1)
    weight_part(2)
    w_sums[2].step(0)
    w_sums[0].step(3)
    normed_grad(1)
    w_sums[1].step(3)
    over.step(0)
    finish()
    dall[0].step(3)
    dall[1].step(2)
    s_sum.step(0)
    w_sums[2].step(1)
    over.step(1)
    dall[2].step(3)
    sout[1].step(2)
    s_sum.step(1)
    w_sums[2].step(2)
    over.step(2)
    over.step(3)
    s_sum.step(2)
    sout[1].step(3)
    dall[1].step(3)
    over.step(4)
    s_sum.step(3)
    spread.step(0)
    w_sums[2].step(3)
    send_parcels()
    spread.step(1)
    spread.step(2)
    sout[1].step(4)
    add_parcels()
    spread.step(3)
    spread.step(4)
    write_out(0)
    write_out(1)
    take_totals()
    for step in range(1, 16):
        parcel(step).wait_send()
        total_message(step).wait_send()
    for copy in owns:
        copy.wait()


def back(tok, cot, seg, turn, wq_all, wo_all, small_t, raw_t, q_t, kv_all, mix_t, lsum, res, ffn, gates_t, share, dx, out_part, dw_own):
    vmem = pl.BlockSpec(memory_space=pltpu.VMEM)
    anywhere = pl.BlockSpec(memory_space=pl.ANY)
    kv_slots = column_slots((4, 128, 128), lead=(2, 2))
    return pl.pallas_call(
        back_kernel,
        out_shape=(
            jax.ShapeDtypeStruct((2, 4, 2, 128, 1024), BF),
            jax.ShapeDtypeStruct((4, 2, 128, 1024), BF),
            jax.ShapeDtypeStruct((2, 128, 1024), BF),
            jax.ShapeDtypeStruct((2, 128, 1024), BF),
            jax.ShapeDtypeStruct((128, 2048), F32),
            jax.ShapeDtypeStruct((128, 1024), F32),
            jax.ShapeDtypeStruct((64, 128), F32),
        ),
        in_specs=[
            vmem, vmem, vmem, anywhere, anywhere, anywhere, vmem, anywhere, vmem, anywhere,
            vmem, vmem, vmem, vmem, vmem, vmem, vmem, anywhere, vmem,
        ],
        out_specs=(anywhere,) * 2 + (vmem,) * 5,
        scratch_shapes=[
            pltpu.VMEM((2, 4, 2, 128, 1024), BF),
            pltpu.VMEM((4, 2, 128, 1024), BF),
            pltpu.VMEM((2, 4, 2, 8, 128, 128), BF),
            pltpu.VMEM((2, 2048, 128), F32),
            pltpu.VMEM((64, 128), F32),
            pltpu.VMEM((2, 1024, 128), BF),
            pltpu.VMEM((2, 128, 1024), F32),
            pltpu.VMEM((256, 1024), BF),
            pltpu.VMEM((2, 1024, 128), BF),
            pltpu.VMEM((2, 1024, 128), F32),
            pltpu.VMEM((2, 8, 128, 128), F32),
            pltpu.VMEM((256, 2048), BF),
            pltpu.VMEM((1024, 256), BF),
            pltpu.VMEM((256, 1024), F32),
            pltpu.VMEM((2, 2, 4, 2, 4, 128, 128), BF),
            pltpu.VMEM((3, 4, 2, 128, 1024), BF),
            pltpu.VMEM((4, 2, 64, 128), F32),
            pltpu.VMEM((64, 128), F32),
            pltpu.VMEM((64, 128), F32),
            *column_slots((128, 1024), lead=(3,)),
            *kv_slots,
            pltpu.VMEM((4, 4, 64, 256), BF),
            pltpu.VMEM((4, 4, 64, 256), BF),
            *scatter_slots(64, 256),
            *column_slots((64, 128), F32),
            pltpu.VMEM((64, 256), BF),
            pltpu.VMEM((64, 1024), BF),
            pltpu.VMEM((64, 1024), F32),
            pltpu.VMEM((4, 4, 128, 1024), BF),
            *scatter_slots(128, 1024),
            pltpu.VMEM((16, 128, 128), BF),
            pltpu.VMEM((16, 128, 128), BF),
            pltpu.VMEM((64, 128), BF),
            pltpu.VMEM((16, 64, 128), BF),
            pltpu.SemaphoreType.DMA((11, 2, 8)),
            pltpu.SemaphoreType.DMA((4, 2, 2, 8)),
            pltpu.SemaphoreType.DMA((16,)),
            pltpu.SemaphoreType.DMA((16,)),
            pltpu.SemaphoreType.DMA((16,)),
            pltpu.SemaphoreType.DMA((16,)),
            pltpu.SemaphoreType.REGULAR,
            pltpu.SemaphoreType.DMA((10,)),
            pltpu.VMEM((8, 1024), F32),
        ],
        compiler_params=pltpu.CompilerParams(
            collective_id=2, has_side_effects=True, vmem_limit_bytes=63 * MIB
        ),
        cost_estimate=pl.CostEstimate(
            flops=12_000_000_000, bytes_accessed=30_000_000, transcendentals=5_000_000
        ),
    )(tok, cot, seg, turn, wq_all, wo_all, small_t, raw_t, q_t, kv_all, mix_t, lsum, res, ffn, gates_t, share, dx, out_part, dw_own)


def last_kernel(
    dgu_ref, dd_ref, out_ref, in_ref, gq_ref, go_ref, gs_ref,
    dgu_f, dd_f, out_f, in_f, gq_f, go_f, attn_f, ffn_f, q_f, k_f, router_f,
):
    dgu_f[...] = dgu_ref[...].astype(F32)
    dd_f[...] = dd_ref[...].astype(F32)
    out_f[...] = out_ref[...]
    in_f[...] = in_ref[...]
    gq_f[...] = gq_ref[...]
    go_f[...] = go_ref[...]
    attn_f[...] = gs_ref[32:33]
    ffn_f[...] = gs_ref[33:34]
    q_f[...] = gs_ref[40:48].T[0:1]
    k_f[...] = gs_ref[48:56].T[0:1]
    router_f[...] = gs_ref[0:32]


def last(dgu, dd, output, in_grad, gq, go, gs):
    def rows(count, width):
        return pl.BlockSpec((count, width), lambda n: (n, 0))

    def whole(*shape):
        return pl.BlockSpec(shape, lambda n: (0, 0))

    return pl.pallas_call(
        last_kernel,
        grid=(8,),
        out_shape=(
            jax.ShapeDtypeStruct((2048, 1024), F32),
            jax.ShapeDtypeStruct((1024, 1024), F32),
            jax.ShapeDtypeStruct((256, 1024), BF),
            jax.ShapeDtypeStruct((256, 1024), BF),
            jax.ShapeDtypeStruct((128, 2048), F32),
            jax.ShapeDtypeStruct((128, 1024), F32),
            jax.ShapeDtypeStruct((1, 128), F32),
            jax.ShapeDtypeStruct((1, 128), F32),
            jax.ShapeDtypeStruct((1, 8), F32),
            jax.ShapeDtypeStruct((1, 8), F32),
            jax.ShapeDtypeStruct((32, 128), F32),
        ),
        in_specs=[
            rows(256, 1024), rows(128, 1024), rows(32, 1024), rows(32, 1024), rows(16, 2048),
            rows(16, 1024), whole(64, 128),
        ],
        out_specs=(
            rows(256, 1024), rows(128, 1024), rows(32, 1024), rows(32, 1024), rows(16, 2048),
            rows(16, 1024), whole(1, 128), whole(1, 128), whole(1, 8), whole(1, 8), whole(32, 128),
        ),
        cost_estimate=pl.CostEstimate(flops=0, bytes_accessed=24_000_000, transcendentals=0),
    )(
        dgu.reshape(2048, 1024), dd.reshape(1024, 1024), output.reshape(256, 1024),
        in_grad.reshape(256, 1024), gq, go, gs,
    )


def turn_table(length):
    frequency = np.power(np.float32(THETA), -2.0 * np.arange(HD // 2, dtype=np.float32) / HD)
    angle = np.arange(length, dtype=np.float32)[:, None] * frequency.astype(np.float32)[None, :]
    both = np.concatenate([np.cos(angle), np.sin(angle)], axis=1).astype(np.float32)
    return both.reshape(length // 128, 128, HD).transpose(0, 2, 1)


def body(
    tokens,
    cotangent,
    segments,
    routes,
    w_qkv,
    w_out,
    attn_norm,
    ffn_norm,
    q_gain,
    k_gain,
    router,
    w_gate_up,
    w_down,
):
    tok = tokens.reshape(2, 128, 1024)
    cot = cotangent.reshape(2, 128, 1024)
    seg = segments.reshape(2, 8, 1, 128)
    routes_t = routes.reshape(2, 128, 8).transpose(0, 2, 1)
    turn = jnp.asarray(turn_table(1024))
    gains = jnp.pad(jnp.stack([q_gain, k_gain]), ((0, 28), (0, 120)))
    small = jnp.concatenate([router.T, attn_norm[None], ffn_norm[None], gains])
    (
        dy_all, x0, wq_all, wo_all, kv_all, raw_t, small_t, q_t, mix_t, lsum, res, ffn, gates_t, sent
    ) = front(tok, cot, w_qkv, w_out, small, seg, routes_t, turn)
    out_part, moved_dx, share, dw_own = moe(ffn, x0, dy_all, sent, w_gate_up, w_down)
    dgu, dd, output, in_grad, gq, go, gs = back(
        tok, cot, seg, turn, wq_all, wo_all, small_t, raw_t, q_t, kv_all, mix_t, lsum, res, ffn,
        gates_t, share, moved_dx, out_part, dw_own,
    )
    dgu, dd, output, in_grad, gq, go, attn, ffn_gain, q_grad, k_grad, router_grad = last(
        dgu, dd, output, in_grad, gq, go, gs
    )
    return (
        output.reshape(tokens.shape),
        in_grad.reshape(tokens.shape),
        gq,
        go,
        attn.reshape(128),
        ffn_gain.reshape(128),
        q_grad.reshape(8),
        k_grad.reshape(8),
        router_grad.T,
        dgu.reshape(2, 1024, 1024),
        dd.reshape(2, 512, 1024),
    )


def solution(mesh):
    return jax.shard_map(
        body,
        mesh=mesh,
        in_specs=(
            P(None, "expert", "dp", None),
            P(None, "expert", "dp", None),
            P(None, "expert", None),
            P(None, "expert", "dp", None),
            P("dp", None),
            P("dp", None),
            P("dp"),
            P("dp"),
            P("dp"),
            P("dp"),
            P("dp", None),
            P("expert", None, None),
            P("expert", None, None),
        ),
        out_specs=(
            P(None, "expert", "dp", None),
            P(None, "expert", "dp", None),
            P("dp", None),
            P("dp", None),
            P("dp"),
            P("dp"),
            P("dp"),
            P("dp"),
            P("dp", None),
            P("expert", None, None),
            P("expert", None, None),
        ),
        check_vma=False,
    )
```

profile of v0, /device:TPU:0, one launch (start us, length us, event | category | flops | bytes accessed | tf_op | source)
XLA Modules:
  0.0 311.6 jit_solution(16326463125630094579)
XLA Ops:
  0.6 0.7 fusion.5
  1.3 1.3 pad_maximum_fusion.small
  2.7 88.5 %shard_map.221 = (bf16[2,4,4,128,1024]{4,3,2,1,0:T(8,128)(2,1)}, bf16[4,4,128,1024]{3,2,1,0:T(8,128)(2,1)}, bf16[2,4,2,128,1024]{4,3,2,1,0:T(8,128)(2,1)}, bf16[...) custom-call(bf16[2,128,1024]{2,1,0:T(8,128)(2,1)} %bitcast.39, ...), custom_call_target="tpu_custom_call" | custom-call | flops 5000000000 | bytes 30000000 | tf_op jit(solution)/shard_map/pallas_call | solution.py:611
  91.2 105.1 %shard_map.222 = (bf16[2,4,4,128,1024]{4,3,2,1,0:T(8,128)(2,1)}, f32[2,128,1024]{2,1,0:T(8,128)}, f32[16,8,128]{2,1,0:T(8,128)}, bf16[3,128,1024]{2,1,0:T(8,128)(2,1)}) custom-call(bf16[2,128,1024]{2,1,0:T(8,128)(2,1)} %get-tuple-element.56.ffn_ref.ffn, bf16[4,4,128,1024]{3,2,1,0:T(8,128)(2,1)} %get-tuple-element.58.x0_hbm, ...), custom_call_target="tpu_custom_call" | custom-call | flops 30000001024 | bytes 30000000 | tf_op jit(solution)/shard_map/pallas_call | solution.py:896
  196.3 105.0 %shard_map.223 = (bf16[2,4,2,128,1024]{4,3,2,1,0:T(8,128)(2,1)}, bf16[4,2,128,1024]{3,2,1,0:T(8,128)(2,1)}, bf16[2,128,1024]{2,1,0:T(8,128)(2,1)}, bf16[2,128,10...) custom-call(bf16[2,128,1024]{2,1,0:T(8,128)(2,1)} %bitcast.40, ...), custom_call_target="tpu_custom_call" | custom-call | flops 12000000000 | bytes 30000000 | tf_op jit(solution)/shard_map/pallas_call | solution.py:1345
  301.3 10.1 %shard_map.224 = (f32[2048,1024]{1,0:T(8,128)}, f32[1024,1024]{1,0:T(8,128)}, bf16[256,1024]{1,0:T(8,128)(2,1)}, bf16[256,1024]{1,0:T(8,128)(2,1)}, f32[128,2048...) custom-call(bf16[2048,1024]{1,0:T(8,128)(2,1)} %bitcast.28, ...), custom_call_target="tpu_custom_call" | custom-call | bytes 24000000 | tf_op jit(solution)/shard_map/pallas_call | solution.py:1439
where the time goes:
time: 312 us
  Pallas kernels  309 us (99%)
    pallas_call x1, Pallas kernels, moe(): pl.pallas_call(moe_kernel, out_shape=(jax.ShapeDtypeStruct((2, 4, 4, 128,...  105 us
    pallas_call x1, Pallas kernels, back(): pl.pallas_call(back_kernel, out_shape=(jax.ShapeDtypeStruct((2, 4, 2, 128...  105 us
    pallas_call x1, Pallas kernels, front(): pl.pallas_call(front_kernel, out_shape=(jax.ShapeDtypeStruct((2, 4, 4, 12...  88.5 us
    pallas_call x1, Pallas kernels, last(): pl.pallas_call(last_kernel, grid=(8,), out_shape=(jax.ShapeDtypeStruct((2...  10.1 us

commit v1 on v0

--- a/solution.py
+++ b/solution.py
@@ -1438,7 +1438,7 @@
 
     return pl.pallas_call(
         last_kernel,
-        grid=(8,),
+        grid=(4,),
         out_shape=(
             jax.ShapeDtypeStruct((2048, 1024), F32),
             jax.ShapeDtypeStruct((1024, 1024), F32),
@@ -1453,13 +1453,14 @@
             jax.ShapeDtypeStruct((32, 128), F32),
         ),
         in_specs=[
-            rows(256, 1024), rows(128, 1024), rows(32, 1024), rows(32, 1024), rows(16, 2048),
-            rows(16, 1024), whole(64, 128),
+            rows(512, 1024), rows(256, 1024), rows(64, 1024), rows(64, 1024), rows(32, 2048),
+            rows(32, 1024), whole(64, 128),
         ],
         out_specs=(
-            rows(256, 1024), rows(128, 1024), rows(32, 1024), rows(32, 1024), rows(16, 2048),
-            rows(16, 1024), whole(1, 128), whole(1, 128), whole(1, 8), whole(1, 8), whole(32, 128),
+            rows(512, 1024), rows(256, 1024), rows(64, 1024), rows(64, 1024), rows(32, 2048),
+            rows(32, 1024), whole(1, 128), whole(1, 128), whole(1, 8), whole(1, 8), whole(32, 128),
         ),
+        compiler_params=pltpu.CompilerParams(vmem_limit_bytes=40 * MIB),
         cost_estimate=pl.CostEstimate(flops=0, bytes_accessed=24_000_000, transcendentals=0),
     )(
         dgu.reshape(2048, 1024), dd.reshape(1024, 1024), output.reshape(256, 1024),

time: 312 us -> 316 us (1.013)
  local copies, waits for them, and re-layouts: 0 us -> 8.88 us
  Pallas kernels: 309 us -> 304 us
    unnamed x0 -> x14, local copies, waits for them, and re-layouts: none -> 8.88 us
    pallas_call x1, Pallas kernels: 10.1 us -> 5.5 us  [last(): pl.pallas_call(last_kernel, grid=(4,), out_shape=(jax.ShapeDtypeStruct((2...]
where the time goes in v1:
time: 316 us
  Pallas kernels  304 us (96%)
  local copies, waits for them, and re-layouts  8.88 us (3%)
    pallas_call x1, Pallas kernels, moe(): pl.pallas_call(moe_kernel, out_shape=(jax.ShapeDtypeStruct((2, 4, 4, 128,...  105 us
    pallas_call x1, Pallas kernels, back(): pl.pallas_call(back_kernel, out_shape=(jax.ShapeDtypeStruct((2, 4, 2, 128...  105 us
    pallas_call x1, Pallas kernels, front(): pl.pallas_call(front_kernel, out_shape=(jax.ShapeDtypeStruct((2, 4, 4, 12...  88.6 us
    unnamed x14, local copies, waits for them, and re-layouts  8.88 us

profile of v1, /device:TPU:0, one launch (start us, length us, event | category | flops | bytes accessed | tf_op | source)
XLA Modules:
  0.0 315.9 jit_solution(16574292729069679058)
XLA Ops:
  0.6 0.7 fusion.5
  1.3 1.3 pad_maximum_fusion.small
  2.7 88.6 %shard_map.221 = (bf16[2,4,4,128,1024]{4,3,2,1,0:T(8,128)(2,1)}, bf16[4,4,128,1024]{3,2,1,0:T(8,128)(2,1)}, bf16[2,4,2,128,1024]{4,3,2,1,0:T(8,128)(2,1)}, bf16[...) custom-call(bf16[2,128,1024]{2,1,0:T(8,128)(2,1)} %bitcast.39, ...), custom_call_target="tpu_custom_call" | custom-call | flops 5000000000 | bytes 30000000 | tf_op jit(solution)/shard_map/pallas_call | solution.py:611
  91.2 105.1 %shard_map.222 = (bf16[2,4,4,128,1024]{4,3,2,1,0:T(8,128)(2,1)}, f32[2,128,1024]{2,1,0:T(8,128)}, f32[16,8,128]{2,1,0:T(8,128)}, bf16[3,128,1024]{2,1,0:T(8,128)(2,1)}) custom-call(bf16[2,128,1024]{2,1,0:T(8,128)(2,1)} %get-tuple-element.56.ffn_ref.ffn, bf16[4,4,128,1024]{3,2,1,0:T(8,128)(2,1)} %get-tuple-element.58.x0_hbm, ...), custom_call_target="tpu_custom_call" | custom-call | flops 30000001024 | bytes 30000000 | tf_op jit(solution)/shard_map/pallas_call | solution.py:896
  196.3 105.0 %shard_map.223 = (bf16[2,4,2,128,1024]{4,3,2,1,0:T(8,128)(2,1)}, bf16[4,2,128,1024]{3,2,1,0:T(8,128)(2,1)}, bf16[2,128,1024]{2,1,0:T(8,128)(2,1)}, bf16[2,128,10...) custom-call(bf16[2,128,1024]{2,1,0:T(8,128)(2,1)} %bitcast.40, ...), custom_call_target="tpu_custom_call" | custom-call | flops 12000000000 | bytes 30000000 | tf_op jit(solution)/shard_map/pallas_call | solution.py:1345
  301.4 0.0 copy-start
  301.4 2.2 copy-done
  303.5 0.0 copy-start.1
  303.5 1.6 copy-done.1
  305.1 0.0 copy-start.2
  305.1 1.2 copy-done.2
  306.4 0.0 copy-start.3
  306.4 1.0 copy-done.3
  307.4 0.0 copy-start.4
  307.4 1.0 copy-done.4
  308.4 0.0 copy-start.5
  308.4 1.0 copy-done.5
  309.5 0.0 copy-start.6
  309.5 0.8 copy-done.6
  310.2 5.5 %shard_map.224 = (f32[2048,1024]{1,0:T(8,128)}, f32[1024,1024]{1,0:T(8,128)}, bf16[256,1024]{1,0:T(8,128)(2,1)}, bf16[256,1024]{1,0:T(8,128)(2,1)}, f32[128,2048...) custom-call(bf16[2048,1024]{1,0:T(8,128)(2,1)S(1)} %bitcast.28, ...), custom_call_target="tpu_custom_call" | custom-call | bytes 24000000 | tf_op jit(solution)/shard_map/pallas_call | solution.py:1439
Async XLA Ops:
  301.4 2.2 copy-start
  303.5 1.6 copy-start.1
  305.1 1.2 copy-start.2
  306.4 1.0 copy-start.3
  307.4 1.0 copy-start.4
  308.4 1.0 copy-start.5
  309.5 0.8 copy-start.6
